TPU v7x, 32 devices: a whole 2x2x4 slice. The times are simulated.
32 devices in a mesh: grp: 2 (over x), tm: 16 (over z, y, core).
Axes of the slice: x: 2, y: 2, z: 4, core: 2. Of those that a mesh axis runs over, the one named last changes fastest.
Arguments:
- launch: float32 [2, 32, 16384], P(None, None, ('grp', 'tm')), parts along dimension 2, may hold values from -6 to 6
- target: float32 [2, 32, 16384], P(None, None, ('grp', 'tm')), parts along dimension 2, may hold values from -4 to 4
- taps: float32 [2, 32, 32, 64], replicated, may hold values from -0.09375 to 0.09375
- coupling: float32 [32, 32], replicated, may hold values from 0.004 to 0.03
- delay: float32 [32], replicated, may hold values from -48 to 48
- curv: float32 [32], replicated, may hold values from -300 to 300
Outputs:
- misfit: float32 [2, 32, 16384], P(None, None, ('grp', 'tm')), parts along dimension 2
- launch_grad: float32 [2, 32, 16384], P(None, None, ('grp', 'tm')), parts along dimension 2
- tap_grad: float32 [4, 32, 32, 64], P('grp'), parts along dimension 0
There are 2 independent parts, one for each index of `grp`. A program takes and returns all parts, laid end to end along the dimension named above; an argument that names none is the same for every part. Nothing has to cross between parts.
All inputs are finite; a program needn't handle non-finite values.
Results may differ from a plain program's by a relative error of at most 0.00028.
Values sent between devices are 32-bit elements; how exact they have to be, the bound alone decides.
A program may use at most 128 MiB of HBM per device.

v0:
```python
import functools
import math

import jax
import jax.numpy as jnp
import ml_dtypes
import numpy as np
from jax import lax
from jax.experimental import pallas as pl
from jax.experimental.pallas import tpu as pltpu
from jax.sharding import PartitionSpec as P


WIN = 8192


def passed_along(block, axis, distance):
    devices = range(lax.axis_size(axis))
    route = [(i - distance, i) for i in devices if i - distance in devices]
    return lax.ppermute(block, axis, route)


def tables(rows, cols, modulus):
    left = jnp.arange(rows, dtype=jnp.int32)[:, None]
    right = jnp.arange(cols, dtype=jnp.int32)[None, :]
    angle = (left * right % modulus).astype(jnp.float32) * (2.0 * math.pi / modulus)
    return (jnp.cos(angle), jnp.sin(angle))


def first_tables(mine, parts, block, total):
    length = parts * block
    index = jnp.arange(length, dtype=jnp.int32)
    outer = index // block
    inner = index % block
    sample = outer[:, None] * length + mine * block + inner[:, None]
    angle = (outer[None, :] * sample % total).astype(jnp.float32) * (2.0 * math.pi / total)
    same = (inner[:, None] == inner[None, :]).astype(jnp.float32)
    return (jnp.cos(angle) * same, jnp.sin(angle) * same)


def rotate(real_part, imag_part, cosine, sine, sign):
    return (
        real_part * cosine - sign * imag_part * sine,
        imag_part * cosine + sign * real_part * sine,
    )


def along_time(field, cosine, sine, sign, form):
    high = lax.Precision.HIGHEST
    cos_real = jnp.einsum(form, field[0], cosine, precision=high)
    cos_imag = jnp.einsum(form, field[1], cosine, precision=high)
    sin_real = jnp.einsum(form, field[0], sine, precision=high)
    sin_imag = jnp.einsum(form, field[1], sine, precision=high)
    return jnp.stack([cos_real - sign * sin_imag, cos_imag + sign * sin_real])


def apply_phase(field, freq, total, delay, curv, sign):
    centred = jnp.where(freq < total // 2, freq, freq - total).astype(jnp.float32) / total
    phase = (
        2.0
        * math.pi
        * (delay[:, None] * centred[None, :] + curv[:, None] * centred[None, :] * centred[None, :])
    )
    first, second = rotate(field[0], field[1], jnp.cos(phase), jnp.sin(phase), sign)
    return jnp.stack([first, second])


def propagate(field, delay, curv, sign):
    two, modes, length = field.shape
    parts = lax.axis_size("tm")
    block = length // parts
    total = length * parts
    mine = lax.axis_index("tm")
    rows = lax.all_to_all(field, "tm", split_axis=2, concat_axis=2, tiled=True)
    cos_first, sin_first = first_tables(mine, parts, block, total)
    rows = along_time(rows, cos_first, sin_first, -1.0, "ms,sk->mk")
    spectra = lax.all_to_all(rows, "tm", split_axis=2, concat_axis=2, tiled=True)
    cos_big, sin_big = tables(length, length, length)
    spectra = along_time(spectra, cos_big, sin_big, -1.0, "ms,sk->mk")
    local = jnp.arange(length, dtype=jnp.int32)
    ordered = lax.all_to_all(spectra, "tm", split_axis=2, concat_axis=2, tiled=True)
    freq = mine * length + local % block * parts + local // block
    ordered = apply_phase(ordered, freq, total, delay, curv, sign)
    spectra = lax.all_to_all(ordered, "tm", split_axis=2, concat_axis=2, tiled=True)
    spectra = along_time(spectra, cos_big, sin_big, 1.0, "ms,sk->mk")
    rows = lax.all_to_all(spectra, "tm", split_axis=2, concat_axis=2, tiled=True)
    rows = along_time(rows, cos_first, sin_first, 1.0, "mk,sk->ms") / total
    return lax.all_to_all(rows, "tm", split_axis=2, concat_axis=2, tiled=True)


def nonlinear(field, coupling):
    power = field[0] * field[0] + field[1] * field[1]
    angle = jnp.dot(coupling, power, precision=lax.Precision.HIGHEST)
    cosine = jnp.cos(angle)
    sine = jnp.sin(angle)
    return jnp.stack([field[0] * cosine - field[1] * sine, field[0] * sine + field[1] * cosine])


def kernel_of(taps):
    upper = jnp.concatenate([taps[0], -taps[1]], axis=1)
    lower = jnp.concatenate([taps[1], taps[0]], axis=1)
    return jnp.concatenate([upper, lower], axis=0)


def per_device(launch, target, taps, coupling, delay, curv):
    two, modes, length = launch.shape
    span = taps.shape[-1] - 1
    moved = propagate(launch, delay, curv, 1.0)
    mixed, nonlinear_pull = jax.vjp(lambda value: nonlinear(value, coupling), moved)
    history = passed_along(mixed[:, :, length - span :], "tm", 1)
    keeper = (lax.axis_index("tm") * length % WIN != 0).astype(jnp.float32)

    def apply_filter(before, own, coeffs):
        joined = jnp.concatenate([before * keeper, own], axis=2).reshape(
            1, two * modes, length + span
        )
        out = lax.conv_general_dilated(
            joined,
            kernel_of(coeffs),
            (1,),
            "VALID",
            dimension_numbers=("NCH", "OIH", "NCH"),
            precision=lax.Precision.HIGHEST,
        )
        return out.reshape(two, modes, length)

    output, filter_pull = jax.vjp(apply_filter, history, mixed, taps)
    misfit = output - target
    grad_before, grad_own, grad_coeffs = filter_pull(misfit)
    returned = passed_along(grad_before, "tm", -1)
    grad_own = grad_own + jnp.concatenate(
        [jnp.zeros((two, modes, length - span), jnp.float32), returned], axis=2
    )
    grad_moved = nonlinear_pull(grad_own)[0]
    launch_grad = propagate(grad_moved, delay, curv, -1.0)
    total = length * lax.axis_size("tm")
    tap_grad = lax.psum(grad_coeffs, "tm") / math.sqrt(total)
    return (misfit, launch_grad, tap_grad)


MESH = pl.DeviceIdType.MESH
LANES = 128
INNER = 8


def halves(table):
    high = table.astype(ml_dtypes.bfloat16)
    low = (table - high.astype(np.float64)).astype(ml_dtypes.bfloat16)
    return high, low


def dft_tables(parts, rows, held):
    count = parts * rows
    total = count * LANES
    k1 = np.arange(count)
    first = np.zeros((2, held, count, parts, held, 2, rows))
    t1 = (np.arange(parts)[:, None] * rows + np.arange(rows)[None, :])
    angle = 2.0 * np.pi * (k1[:, None, None] * t1[None] % count) / count
    wide = np.zeros((parts, held, 2, rows + 2, 2, held, count))
    t1w = np.arange(parts)[:, None] * rows + np.arange(rows + 2)[None, :] - 1
    inside = ((t1w >= 0) & (t1w < count)).astype(np.float64)
    anglew = 2.0 * np.pi * (t1w[:, :, None] * k1[None, None, :] % count) / count
    cosw, sinw = np.cos(anglew) * inside[:, :, None], np.sin(anglew) * inside[:, :, None]
    for m in range(held):
        first[0, m, :, :, m, 0, :] = np.cos(angle)
        first[0, m, :, :, m, 1, :] = np.sin(angle)
        first[1, m, :, :, m, 0, :] = -np.sin(angle)
        first[1, m, :, :, m, 1, :] = np.cos(angle)
        wide[:, m, 0, :, 0, m, :] = cosw
        wide[:, m, 0, :, 1, m, :] = -sinw
        wide[:, m, 1, :, 0, m, :] = sinw
        wide[:, m, 1, :, 1, m, :] = cosw
    size = 2 * held * count
    first = first.reshape(size, size)
    wide = wide.reshape(parts * held * 2 * (rows + 2), size)
    lane = np.arange(LANES)
    inner = 2.0 * np.pi * (lane[:, None] * lane[None, :] % LANES) / LANES
    cosine, sine = np.cos(inner), np.sin(inner)
    second = np.block([[cosine, -sine], [sine, cosine]])
    twist = 2.0 * np.pi * (k1[:, None] * lane[None, :]) / total
    freq = k1[:, None] + count * lane[None, :]
    centred = np.where(freq < total // 2, freq, freq - total) / total
    stack = lambda value: np.tile(value, (held, 1)).astype(np.float32)
    big = []
    for table in (first, first.T, wide, second, second.T):
        big += list(halves(np.ascontiguousarray(table)))
    return tuple(big) + (stack(np.cos(twist)), stack(np.sin(twist)), stack(centred))


def split(value):
    high = value.astype(jnp.bfloat16)
    return high, (value - high.astype(jnp.float32)).astype(jnp.bfloat16)


def dot3(left, right, dims=(((1,), (0,)), ((), ()))):
    one = functools.partial(lax.dot_general, dimension_numbers=dims, preferred_element_type=jnp.float32)
    return one(left[0], right[0]) + (one(left[0], right[1]) + one(left[1], right[0]))


SIN = [(-1) ** i * (2.0 * math.pi) ** (2 * i + 1) / math.factorial(2 * i + 1) for i in range(8)]
COS = [(-1) ** i * (2.0 * math.pi) ** (2 * i) / math.factorial(2 * i) for i in range(8)]


def circle(turns):
    quarter = jnp.round(turns * 4.0)
    rest = turns - quarter * 0.25
    square = rest * rest
    sine = jnp.full_like(rest, SIN[5])
    cosine = jnp.full_like(rest, COS[6])
    for i in range(4, -1, -1):
        sine = sine * square + SIN[i]
    for i in range(5, -1, -1):
        cosine = cosine * square + COS[i]
    sine = sine * rest
    which = quarter - 4.0 * jnp.floor(quarter * 0.25)
    odd = (which == 1.0) | (which == 3.0)
    cos_sign = jnp.where((which == 1.0) | (which == 2.0), -1.0, 1.0)
    sin_sign = jnp.where(which >= 2.0, -1.0, 1.0)
    return jnp.where(odd, sine, cosine) * cos_sign, jnp.where(odd, cosine, sine) * sin_sign


def kernel(
    parts, launch, target, a_in, b_in, coupling, coupling_t, delay, curv,
    f_h, f_l, ft_h, ft_l, wd_h, wd_l, s_h, s_l, st_h, st_l, tw_c, tw_s, grid_q,
    misfit_out, grad_out, tap_out,
    send1, recv1, send2, recv2, send3, recv3, send4, recv4, edge_send, edge, taps_own, rs1, half, rs2, mine_sum, gathered,
    a_h, a_l, b_h, b_l, x_h, x_l, prod, mc_h, mc_l, y_h, y_l,
    s_sem, r_sem, es_sem, er_sem, c_ssem, c_rsem,
):
    two, modes, length = launch.shape
    rows = length // LANES
    wide = rows + 2
    held = modes // parts
    count = parts * rows
    me = lax.axis_index("tm")
    chips = parts // 2
    chip, core = me // 2, me % 2
    sibling = chip * 2 + (1 - core)

    def at(index):
        return {"tm": index}

    def remote(source, dest, ssem, rsem, device):
        return pltpu.make_async_remote_copy(
            src_ref=source, dst_ref=dest, send_sem=ssem, recv_sem=rsem, device_id=at(device), device_id_type=MESH
        )

    def rows_of(ref, index, size):
        return ref.at[pl.ds(pl.multiple_of(index * size, 8), size), :]

    def exchange(phase, source, dest, size):
        def go(k, carry):
            other = lax.rem(me + k, parts)
            remote(rows_of(source, other, size), rows_of(dest, me, size), s_sem.at[phase, other], r_sem.at[phase, me], other).start()
            return carry

        lax.fori_loop(1, parts, go, 0)
        own = pl.ds(pl.multiple_of(me * size, 8), size)
        dest[own, :] = source[own, :]

    def arrive(phase, source, dest, size):
        def go(k, carry):
            other = lax.rem(me + parts - k, parts)
            remote(rows_of(source, other, size), rows_of(dest, other, size), s_sem.at[phase, other], r_sem.at[phase, other], other).wait_recv()
            return carry

        lax.fori_loop(1, parts, go, 0)

    def sent(phase, source, dest, size):
        def go(k, carry):
            other = lax.rem(me + k, parts)
            remote(rows_of(source, other, size), rows_of(dest, other, size), s_sem.at[phase, other], r_sem.at[phase, other], other).wait_send()
            return carry

        lax.fori_loop(1, parts, go, 0)

    barrier = pltpu.get_barrier_semaphore()

    def greet(k, carry):
        pl.semaphore_signal(barrier, inc=1, device_id=at(lax.rem(me + k, parts)), device_id_type=MESH)
        return carry

    lax.fori_loop(1, parts, greet, 0)
    for c in range(2):
        for r in range(rows):
            send1[pl.ds(c * rows + r, modes, stride=2 * rows), :] = launch[c, :, r * LANES : (r + 1) * LANES]
        edge_send[c * modes : (c + 1) * modes, :] = target[c, :, :LANES]
    pl.semaphore_wait(barrier, parts - 1)

    block = 2 * held * rows
    block_wide = 2 * held * wide
    exchange(0, send1, recv1, block)
    before, after = lax.rem(me + parts - 1, parts), lax.rem(me + 1, parts)
    edge_copy = remote(edge_send, edge, es_sem, er_sem, before)
    edge_copy.start()

    band = lax.broadcasted_iota(jnp.int32, (held * count, LANES), 0) // count
    q = grid_q[...]
    slope = jnp.zeros((held * count, LANES), jnp.float32)
    bend = jnp.zeros((held * count, LANES), jnp.float32)
    for m in range(held):
        slope = jnp.where(band == m, delay[me * held + m], slope)
        bend = jnp.where(band == m, curv[me * held + m], bend)
    phase_c, phase_s = circle(slope * q + bend * q * q)
    scale = 1.0 / (count * LANES)
    phase_c = phase_c * scale
    phase_s = phase_s * scale
    for source, high, low in ((a_in, a_h, a_l), (b_in, b_h, b_l)):
        high[...], low[...] = split(source[...])
    tc, ts = tw_c[...], tw_s[...]
    half_rows = held * count

    def disperse(received, sign, back_h, back_l):
        y = dot3((f_h[...], f_l[...]), split(received[...]))
        yr, yi = y[:half_rows], y[half_rows:]
        y = jnp.concatenate([yr * tc + yi * ts, yi * tc - yr * ts], axis=1)
        z = dot3(split(y), (s_h[...], s_l[...]))
        zr, zi = z[:, :LANES], z[:, LANES:]
        z = jnp.concatenate([zr * phase_c - sign * (zi * phase_s), zi * phase_c + sign * (zr * phase_s)], axis=1)
        u = dot3(split(z), (st_h[...], st_l[...]))
        ur, ui = u[:, :LANES], u[:, LANES:]
        u = jnp.concatenate([ur * tc - ui * ts, ui * tc + ur * ts], axis=0)
        return dot3((back_h[...], back_l[...]), split(u))

    arrive(0, send1, recv1, block)
    send2[...] = disperse(recv1, 1.0, wd_h, wd_l)
    exchange(1, send2, recv2, block_wide)
    arrive(1, send2, recv2, block_wide)

    def lanes_of(ref, c, span):
        return jnp.concatenate([ref[pl.ds(c * span + r, modes, stride=2 * span), :] for r in range(span)], axis=1)

    vr, vi = lanes_of(recv2, 0, wide), lanes_of(recv2, 1, wide)
    angle = dot3(split(coupling[...]), split(vr * vr + vi * vi))
    cosine, sine = circle(angle * (0.5 / math.pi))
    w = (vr * cosine - vi * sine, vr * sine + vi * cosine)
    full = wide * LANES
    ext = (rows + 1) * LANES
    outer = a_in.shape[0] // (2 * modes)
    span = outer * INNER

    for c in range(2):
        for j in range(INNER):
            moved = pltpu.roll(w[c], full - (LANES - span + j), 1)[:, :ext]
            high, low = split(moved)
            place = (slice(j * modes, (j + 1) * modes), slice(c * ext, (c + 1) * ext))
            x_h[place] = high
            x_l[place] = low
    prod[...] = dot3((a_h[...], a_l[...]), (x_h[...], x_l[...]))
    yr = jnp.zeros((modes, ext), jnp.float32)
    yi = jnp.zeros((modes, ext), jnp.float32)
    for b in range(outer):
        base = b * 2 * modes
        rr = prod[base : base + modes, :ext] - prod[base + modes : base + 2 * modes, ext:]
        ri = prod[base : base + modes, ext:] + prod[base + modes : base + 2 * modes, :ext]
        yr = yr + pltpu.roll(rr, ext - (INNER * b + 1), 1)
        yi = yi + pltpu.roll(ri, ext - (INNER * b + 1), 1)
    remote(edge_send, edge, es_sem, er_sem, after).wait_recv()
    lane = lax.broadcasted_iota(jnp.int32, (modes, LANES), 1)
    keep = (lane < span) & (me != parts - 1)
    m = []
    for c, y in ((0, yr), (1, yi)):
        own = y[:, :length] - target[c]
        misfit_out[c] = own
        m.append((own, jnp.where(keep, y[:, length:] - edge[c * modes : (c + 1) * modes, :], 0.0)))

    zero = jnp.zeros((modes, LANES), jnp.float32)
    own = [jnp.concatenate([part[0], zero], axis=1) for part in m]
    for b in range(outer):
        base = b * 2 * modes
        first = split(pltpu.roll(own[0], INNER * b + 1, 1))
        second = split(pltpu.roll(own[1], INNER * b + 1, 1))
        for ref, one, two_ in ((mc_h, first[0], second[0]), (mc_l, first[1], second[1])):
            ref[base : base + modes, :ext] = one
            ref[base : base + modes, ext:] = two_
            ref[base + modes : base + 2 * modes, :ext] = two_
            ref[base + modes : base + 2 * modes, ext:] = -one
    taps_own[...] = dot3((mc_h[...], mc_l[...]), (x_h[...], x_l[...]), (((1,), (1,)), ((), ())))
    half_size = taps_own.shape[0] // 2
    piece = half_size // chips
    swap = remote(rows_of(taps_own, 1 - core, half_size), rs1, c_ssem.at[0], c_rsem.at[0], sibling)
    swap.start()

    joined = [jnp.concatenate(part, axis=1) for part in m]
    for c in range(2):
        for j in range(INNER):
            moved = joined[c] if j == INNER - 1 else pltpu.roll(joined[c], ext - (INNER - 1 - j), 1)
            high, low = split(moved)
            place = (slice(j * modes, (j + 1) * modes), slice(c * ext, (c + 1) * ext))
            y_h[place] = high
            y_l[place] = low
    prod[...] = dot3((b_h[...], b_l[...]), (y_h[...], y_l[...]))

    swap.wait_recv()
    half[...] = taps_own[pl.ds(pl.multiple_of(core * half_size, 8), half_size), :] + rs1[...]

    def scatter(k, carry):
        other = lax.rem(chip + k, chips)
        remote(rows_of(half, other, piece), rows_of(rs2, chip, piece), c_ssem.at[1 + other], c_rsem.at[1 + chip], other * 2 + core).start()
        return carry

    lax.fori_loop(1, chips, scatter, 0)

    gr = jnp.zeros((modes, length), jnp.float32)
    gi = jnp.zeros((modes, length), jnp.float32)
    for b in range(outer):
        base = b * 2 * modes
        rr = prod[base : base + modes, :ext] + prod[base + modes : base + 2 * modes, ext:]
        ri = prod[base : base + modes, ext:] - prod[base + modes : base + 2 * modes, :ext]
        shift = span - INNER - INNER * b
        if shift:
            rr = pltpu.roll(rr, ext - shift, 1)
            ri = pltpu.roll(ri, ext - shift, 1)
        gr = gr + rr[:, :length]
        gi = gi + ri[:, :length]
    here = slice(LANES, LANES + length)
    wr, wi, cosine, sine = w[0][:, here], w[1][:, here], cosine[:, here], sine[:, here]
    pull = dot3(split(coupling_t[...]), split(gi * wr - gr * wi)) * 2.0
    vr = gr * cosine + gi * sine + vr[:, here] * pull
    vi = gi * cosine - gr * sine + vi[:, here] * pull
    for c, value in ((0, vr), (1, vi)):
        for r in range(rows):
            send3[pl.ds(c * rows + r, modes, stride=2 * rows), :] = value[:, r * LANES : (r + 1) * LANES]
    exchange(2, send3, recv3, block)
    arrive(2, send3, recv3, block)
    send4[...] = disperse(recv3, -1.0, ft_h, ft_l)
    exchange(3, send4, recv4, block)

    def scattered(k, carry):
        other = lax.rem(chip + chips - k, chips)
        remote(rows_of(half, other, piece), rows_of(rs2, other, piece), c_ssem.at[1 + other], c_rsem.at[1 + other], other * 2 + core).wait_recv()
        return carry

    lax.fori_loop(1, chips, scattered, 0)
    own_piece = pl.ds(pl.multiple_of(chip * piece, 8), piece)
    rs2[own_piece, :] = half[own_piece, :]
    total = rs2[:piece, :]
    for k in range(1, chips):
        total = total + rs2[k * piece : (k + 1) * piece, :]
    mine_sum[...] = total * (1.0 / math.sqrt(count * LANES))
    base = 1 + chips

    def slot(c_, k_):
        return rows_of(gathered, c_ * chips + k_, piece)

    def spread(k, carry):
        other = lax.rem(chip + k, chips)
        remote(mine_sum, slot(core, chip), c_ssem.at[base + other], c_rsem.at[base + chip], other * 2 + core).start()
        return carry

    lax.fori_loop(1, chips, spread, 0)
    base2 = base + chips
    remote(mine_sum, slot(core, chip), c_ssem.at[base2 + chip], c_rsem.at[base2 + chip], sibling).start()
    gathered[pl.ds(pl.multiple_of((core * chips + chip) * piece, 8), piece), :] = mine_sum[...]

    arrive(3, send4, recv4, block)
    for c in range(2):
        grad_out[c] = lanes_of(recv4, c, rows)

    def pass_on(k, carry):
        other = lax.rem(chip + chips - k, chips)
        remote(mine_sum, slot(core, other), c_ssem.at[base + other], c_rsem.at[base + other], other * 2 + core).wait_recv()
        remote(slot(core, other), slot(core, other), c_ssem.at[base2 + other], c_rsem.at[base2 + other], sibling).start()
        return carry

    lax.fori_loop(1, chips, pass_on, 0)

    def collect(k, carry):
        other = lax.rem(chip + chips - k, chips)
        remote(slot(1 - core, other), slot(1 - core, other), c_ssem.at[base2 + other], c_rsem.at[base2 + other], sibling).wait_recv()
        return carry

    lax.fori_loop(0, chips, collect, 0)
    tap_out[...] = gathered[...]

    edge_copy.wait_send()
    swap.wait_send()
    sent(0, send1, recv1, block)
    sent(1, send2, recv2, block_wide)
    sent(2, send3, recv3, block)
    sent(3, send4, recv4, block)

    def left(k, carry):
        other = lax.rem(chip + k, chips)
        remote(rows_of(half, other, piece), rows_of(rs2, other, piece), c_ssem.at[1 + other], c_rsem.at[1 + other], sibling).wait_send()
        remote(mine_sum, slot(core, other), c_ssem.at[base + other], c_rsem.at[base + other], sibling).wait_send()
        return carry

    lax.fori_loop(1, chips, left, 0)

    def handed(k, carry):
        other = lax.rem(chip + chips - k, chips)
        remote(slot(core, other), slot(core, other), c_ssem.at[base2 + other], c_rsem.at[base2 + other], sibling).wait_send()
        return carry

    lax.fori_loop(1, chips, handed, 0)
    remote(mine_sum, slot(core, chip), c_ssem.at[base2 + chip], c_rsem.at[base2 + chip], sibling).wait_send()


def fused(launch, target, taps, coupling, delay, curv):
    two, modes, length = launch.shape
    parts = lax.axis_size("tm")
    span = taps.shape[-1]
    outer = span // INNER
    rows = length // LANES
    held = modes // parts
    wide = (rows + 2) * parts * held * 2
    plain = rows * parts * held * 2
    ext = (rows + 1) * LANES
    chips = parts // 2
    pieces = taps.reshape(2, modes, modes, outer, INNER)
    forward = pieces.transpose(3, 0, 1, 4, 2).reshape(outer * 2 * modes, INNER * modes)
    backward = pieces.transpose(3, 0, 2, 4, 1).reshape(outer * 2 * modes, INNER * modes)
    size = outer * 2 * modes
    cols = INNER * modes
    tables_ = [jnp.asarray(table) for table in dft_tables(parts, rows, held)]
    vmem = pl.BlockSpec(memory_space=pltpu.VMEM)
    smem = pl.BlockSpec(memory_space=pltpu.SMEM)
    f32, bf16 = jnp.float32, jnp.bfloat16
    field = lambda n: pltpu.VMEM((n, LANES), f32)
    misfit, launch_grad, tap = pl.pallas_call(
        functools.partial(kernel, parts),
        out_shape=(
            jax.ShapeDtypeStruct((2, modes, length), f32),
            jax.ShapeDtypeStruct((2, modes, length), f32),
            jax.ShapeDtypeStruct((size, cols), f32),
        ),
        in_specs=[vmem] * 6 + [smem] * 2 + [vmem] * len(tables_),
        out_specs=(vmem, vmem, vmem),
        scratch_shapes=[
            field(plain), field(plain), field(wide), field(wide), field(plain), field(plain), field(plain), field(plain),
            field(2 * modes), field(2 * modes),
            pltpu.VMEM((size, cols), f32), pltpu.VMEM((size // 2, cols), f32), pltpu.VMEM((size // 2, cols), f32),
            pltpu.VMEM((size // 2, cols), f32), pltpu.VMEM((size // parts, cols), f32), pltpu.VMEM((size, cols), f32),
            pltpu.VMEM((size, cols), bf16), pltpu.VMEM((size, cols), bf16),
            pltpu.VMEM((size, cols), bf16), pltpu.VMEM((size, cols), bf16),
            pltpu.VMEM((cols, 2 * ext), bf16), pltpu.VMEM((cols, 2 * ext), bf16),
            pltpu.VMEM((size, 2 * ext), f32),
            pltpu.VMEM((size, 2 * ext), bf16), pltpu.VMEM((size, 2 * ext), bf16),
            pltpu.VMEM((cols, 2 * ext), bf16), pltpu.VMEM((cols, 2 * ext), bf16),
            pltpu.SemaphoreType.DMA((4, parts)), pltpu.SemaphoreType.DMA((4, parts)),
            pltpu.SemaphoreType.DMA, pltpu.SemaphoreType.DMA,
            pltpu.SemaphoreType.DMA((1 + 3 * chips,)), pltpu.SemaphoreType.DMA((1 + 3 * chips,)),
        ],
        compiler_params=pltpu.CompilerParams(collective_id=0, has_side_effects=True, vmem_limit_bytes=48 * 1024 * 1024),
    )(launch, target, forward, backward, coupling, coupling.T, delay, curv, *tables_)
    tap = tap.reshape(outer, 2, modes, INNER, modes).transpose(1, 2, 4, 0, 3).reshape(taps.shape)
    return misfit, launch_grad, tap


def fits(launch, taps, parts):
    two, modes, length = launch.shape
    return (
        parts % 2 == 0
        and parts > 2
        and modes % parts == 0
        and modes % 16 == 0
        and length % LANES == 0
        and length * parts == WIN
        and taps.shape[-1] % INNER == 0
        and taps.shape[-1] < LANES
        and (2 * (modes // parts) * (length // LANES)) % 8 == 0
        and (2 * (modes // parts) * (length // LANES + 2)) % 8 == 0
    )


def choose(launch, target, taps, coupling, delay, curv):
    if fits(launch, taps, lax.axis_size("tm")):
        return fused(launch, target, taps, coupling, delay, curv)
    return per_device(launch, target, taps, coupling, delay, curv)


def solution(mesh):
    in_specs = (P(None, None, ("grp", "tm")), P(None, None, ("grp", "tm")), P(), P(), P(), P())
    out_specs = (
        P(None, None, ("grp", "tm")),
        P(None, None, ("grp", "tm")),
        P("grp", None, None, None),
    )
    return jax.shard_map(
        choose, mesh=mesh, in_specs=in_specs, out_specs=out_specs, check_vma=False
    )
```

profile of v0, /device:TPU:1, one launch (start us, length us, event | category | flops | bytes accessed | tf_op | source)
XLA Modules:
  0.0 72.5 jit_solution(16061108125847121199)
XLA Ops:
  0.6 1.8 %copy.26 = f32[2,32,32,64]{2,3,1,0:T(8,128)S(1)} copy(f32[2,32,32,64]{3,2,1,0:T(8,128)} %param.21) | data formatting | bytes 1048576 | tf_op args[2]
  2.5 1.6 %copy.27 = f32[8,2,32,8,32]{4,3,2,1,0:T(8,128)} copy(f32[8,2,32,8,32]{4,3,0,2,1:T(8,128)S(1)} %bitcast.16) | data formatting | bytes 1048576 | tf_op jit(solution)/shard_map/transpose | solution.py:512
  4.0 2.1 %reshape.22.a_in = f32[512,256]{1,0:T(8,128)S(1)} reshape(f32[8,2,32,8,32]{4,3,2,1,0:T(8,128)} %copy.27) | data formatting | bytes 1048576 | tf_op jit(solution)/shard_map/reshape | solution.py:512
  6.2 2.4 %copy.28 = f32[8,2,32,8,32]{4,3,2,1,0:T(8,128)} copy(f32[8,2,32,8,32]{2,3,0,4,1:T(8,128)S(1)} %bitcast.17) | data formatting | bytes 1048576 | tf_op jit(solution)/shard_map/transpose | solution.py:513
  8.6 0.0 copy-start.5
  8.6 0.0 copy-start.6
  8.6 0.0 copy-start.7
  8.6 0.0 copy-start.8
  8.7 0.0 copy-start.10
  8.7 0.0 copy-start.11
  8.7 2.3 %reshape.23.b_in = f32[512,256]{1,0:T(8,128)S(1)} reshape(f32[8,2,32,8,32]{4,3,2,1,0:T(8,128)} %copy.28) | data formatting | bytes 1048576 | tf_op jit(solution)/shard_map/reshape | solution.py:513
  11.0 0.7 copy.29
  11.8 0.7 copy-done.13
  12.5 0.8 %copy-done.14 = f32[128,128]{1,0:T(8,128)S(1)} copy-done((f32[128,128]{1,0:T(8,128)S(1)}, f32[128,128]{1,0:T(8,128)}, u32[]{:S(2)}) %copy-start.14) | copy-done | bytes 65560
  13.3 0.8 %copy-done.15 = f32[128,128]{1,0:T(8,128)S(1)} copy-done((f32[128,128]{1,0:T(8,128)S(1)}, f32[128,128]{1,0:T(8,128)}, u32[]{:S(2)}) %copy-start.15) | copy-done | bytes 65560
  14.2 0.8 %copy-done.16 = f32[128,128]{1,0:T(8,128)S(1)} copy-done((f32[128,128]{1,0:T(8,128)S(1)}, f32[128,128]{1,0:T(8,128)}, u32[]{:S(2)}) %copy-start.16) | copy-done | bytes 65560
  15.0 0.7 copy-done.17
  15.7 0.7 copy-done.18
  16.3 49.6 %shard_map.202 = (f32[2,32,512]{2,1,0:T(8,128)S(1)}, f32[2,32,512]{2,1,0:T(8,128)S(1)}, f32[512,256]{1,0:T(8,128)S(1)}) custom-call(f32[2,32,512]{2,1,0:T(8,128)S(1)} %copy-done.2, f32[2,32,512]{2,1,0:T(8,128)S(1)} %copy-done.3, f32[512,256]{1,0:T(8,128)S(1)} %reshape.22.a_in, f32[512,256]{1,0:T(8,128)S(1)} %reshape.23.b_in, f32[32,32]{1,0:T(8,128)S(1)} %copy-done.12, ...), custom_call_target="tpu_custom_call" | custom-call | tf_op jit(solution)/shard_map/pallas_call | solution.py:521
  65.9 0.5 reshape.24
  66.4 1.6 %copy.33 = f32[8,2,32,8,32]{4,3,0,2,1:T(8,128)} copy(f32[8,2,32,8,32]{4,3,2,1,0:T(8,128)S(1)} %reshape.24) | data formatting | bytes 1048576 | tf_op jit(solution)/shard_map/reshape | solution.py:547
  68.0 3.2 %copy.31 = f32[2,32,32,64]{3,2,1,0:T(8,128)} copy(f32[2,32,32,64]{2,3,1,0:T(8,128)} %bitcast.18) | data formatting | bytes 1048576
  71.2 0.7 copy.36
  71.8 0.7 copy.37
  (26 shorter events, 0.1 us)
Async XLA Ops:
  8.6 2.4 %copy-start.12 = (f32[32,32]{1,0:T(8,128)S(1)}, f32[32,32]{1,0:T(8,128)}, u32[]{:S(2)}) copy-start(f32[32,32]{1,0:T(8,128)} %coupling.1) | copy-start | bytes 12292
  8.6 3.1 %copy-start = (bf16[384,256]{1,0:T(8,128)(2,1)S(1)}, bf16[384,256]{1,0:T(8,128)(2,1)}, u32[]{:S(2)}) copy-start(bf16[384,256]{1,0:T(8,128)(2,1)} %constant.30.clone.wd_h) | copy-start | bytes 589828
  8.6 3.1 %copy-start.1 = (bf16[384,256]{1,0:T(8,128)(2,1)S(1)}, bf16[384,256]{1,0:T(8,128)(2,1)}, u32[]{:S(2)}) copy-start(bf16[384,256]{1,0:T(8,128)(2,1)} %constant.31.clone.wd_l) | copy-start | bytes 589828
  8.6 3.1 %copy-start.2 = (f32[2,32,512]{2,1,0:T(8,128)S(1)}, f32[2,32,512]{2,1,0:T(8,128)}, u32[]{:S(2)}) copy-start(f32[2,32,512]{2,1,0:T(8,128)} %launch.1) | copy-start | bytes 393220
  8.6 3.1 %copy-start.3 = (f32[2,32,512]{2,1,0:T(8,128)S(1)}, f32[2,32,512]{2,1,0:T(8,128)}, u32[]{:S(2)}) copy-start(f32[2,32,512]{2,1,0:T(8,128)} %target.1) | copy-start | bytes 393220
  8.6 3.1 %copy-start.4 = (bf16[256,256]{1,0:T(8,128)(2,1)S(1)}, bf16[256,256]{1,0:T(8,128)(2,1)}, u32[]{:S(2)}) copy-start(bf16[256,256]{1,0:T(8,128)(2,1)} %constant.26.clone.f_h) | copy-start | bytes 393220
  8.6 3.1 %copy-start.5 = (bf16[256,256]{1,0:T(8,128)(2,1)S(1)}, bf16[256,256]{1,0:T(8,128)(2,1)}, u32[]{:S(2)}) copy-start(bf16[256,256]{1,0:T(8,128)(2,1)} %constant.27.clone.f_l) | copy-start | bytes 393220
  8.6 3.1 %copy-start.6 = (bf16[256,256]{1,0:T(8,128)(2,1)S(1)}, bf16[256,256]{1,0:T(8,128)(2,1)}, u32[]{:S(2)}) copy-start(bf16[256,256]{1,0:T(8,128)(2,1)} %constant.28.clone.ft_h) | copy-start | bytes 393220
  8.6 3.1 %copy-start.7 = (bf16[256,256]{1,0:T(8,128)(2,1)S(1)}, bf16[256,256]{1,0:T(8,128)(2,1)}, u32[]{:S(2)}) copy-start(bf16[256,256]{1,0:T(8,128)(2,1)} %constant.29.clone.ft_l) | copy-start | bytes 393220
  8.6 3.1 %copy-start.8 = (bf16[256,256]{1,0:T(8,128)(2,1)S(1)}, bf16[256,256]{1,0:T(8,128)(2,1)}, u32[]{:S(2)}) copy-start(bf16[256,256]{1,0:T(8,128)(2,1)} %constant.32.clone.s_h) | copy-start | bytes 393220
  8.6 3.1 %copy-start.9 = (bf16[256,256]{1,0:T(8,128)(2,1)S(1)}, bf16[256,256]{1,0:T(8,128)(2,1)}, u32[]{:S(2)}) copy-start(bf16[256,256]{1,0:T(8,128)(2,1)} %constant.33.clone.s_l) | copy-start | bytes 393220
  8.7 3.1 %copy-start.10 = (bf16[256,256]{1,0:T(8,128)(2,1)S(1)}, bf16[256,256]{1,0:T(8,128)(2,1)}, u32[]{:S(2)}) copy-start(bf16[256,256]{1,0:T(8,128)(2,1)} %constant.34.clone.st_h) | copy-start | bytes 393220
  8.7 3.1 %copy-start.11 = (bf16[256,256]{1,0:T(8,128)(2,1)S(1)}, bf16[256,256]{1,0:T(8,128)(2,1)}, u32[]{:S(2)}) copy-start(bf16[256,256]{1,0:T(8,128)(2,1)} %constant.35.clone.st_l) | copy-start | bytes 393220
  11.8 0.7 copy-start.13
  12.5 0.8 %copy-start.14 = (f32[128,128]{1,0:T(8,128)S(1)}, f32[128,128]{1,0:T(8,128)}, u32[]{:S(2)}) copy-start(f32[128,128]{1,0:T(8,128)} %constant.36.clone.tw_c) | copy-start | bytes 196612
  13.3 0.8 %copy-start.15 = (f32[128,128]{1,0:T(8,128)S(1)}, f32[128,128]{1,0:T(8,128)}, u32[]{:S(2)}) copy-start(f32[128,128]{1,0:T(8,128)} %constant.37.clone.tw_s) | copy-start | bytes 196612
  14.2 0.8 %copy-start.16 = (f32[128,128]{1,0:T(8,128)S(1)}, f32[128,128]{1,0:T(8,128)}, u32[]{:S(2)}) copy-start(f32[128,128]{1,0:T(8,128)} %constant.38.clone.grid_q) | copy-start | bytes 196612
  15.0 0.7 copy-start.17
  15.7 0.7 copy-start.18
where the time goes:
time: 72.9 us; the launch traced here: 72.5 us
  Pallas kernels  49.6 us (68%)
  local copies, waits for them, and re-layouts  22.1 us (30%)
  between operations  0.84 us (1%)
    pallas_call x1, Pallas kernels, fused(): pl.pallas_call(functools.partial(kernel, parts), out_shape=(jax.ShapeDtyp...  49.6 us
    unnamed x43, local copies, waits for them, and re-layouts  11.6 us
    transpose x1, local copies, waits for them, and re-layouts, fused(): pieces.transpose(3, 0, 2, 4, 1).reshape(outer * 2 * modes, INNER * modes)  2.38 us
    reshape x1, local copies, waits for them, and re-layouts, fused(): pieces.transpose(3, 0, 2, 4, 1).reshape(outer * 2 * modes, INNER * modes)  2.31 us
    reshape x1, local copies, waits for them, and re-layouts, fused(): pieces.transpose(3, 0, 1, 4, 2).reshape(outer * 2 * modes, INNER * modes)  2.13 us
    reshape x2, local copies, waits for them, and re-layouts, fused(): tap.reshape(outer, 2, modes, INNER, modes).transpose(1, 2, 4, 0, 3)  2.1 us
    transpose x1, local copies, waits for them, and re-layouts, fused(): pieces.transpose(3, 0, 1, 4, 2).reshape(outer * 2 * modes, INNER * modes)  1.55 us

commit v1 on v0

--- a/solution.py
+++ b/solution.py
@@ -141,6 +141,7 @@
 MESH = pl.DeviceIdType.MESH
 LANES = 128
 INNER = 8
+TABLES = 13
 
 
 def halves(table):
@@ -220,13 +221,17 @@
 
 
 def kernel(
-    parts, launch, target, a_in, b_in, coupling, coupling_t, delay, curv,
-    f_h, f_l, ft_h, ft_l, wd_h, wd_l, s_h, s_l, st_h, st_l, tw_c, tw_s, grid_q,
-    misfit_out, grad_out, tap_out,
+    parts, launch, target, coupling, delay, curv, taps_far, *rest,
+):
+    far, rest = rest[:TABLES], rest[TABLES:]
+    misfit_out, grad_out, tap_out = rest[:3]
+    taps_in, *near = rest[3 : 4 + TABLES]
+    (f_h, f_l, ft_h, ft_l, wd_h, wd_l, s_h, s_l, st_h, st_l, tw_c, tw_s, grid_q) = near
+    (
     send1, recv1, send2, recv2, send3, recv3, send4, recv4, edge_send, edge, taps_own, rs1, half, rs2, mine_sum, gathered,
-    a_h, a_l, b_h, b_l, x_h, x_l, prod, mc_h, mc_l, y_h, y_l,
-    s_sem, r_sem, es_sem, er_sem, c_ssem, c_rsem,
-):
+    turned, a_f, a_h, a_l, b_h, b_l, x_h, x_l, prod, mc_h, mc_l, grad_w,
+    s_sem, r_sem, es_sem, er_sem, c_ssem, c_rsem, l_sem,
+    ) = rest[4 + TABLES :]
     two, modes, length = launch.shape
     rows = length // LANES
     wide = rows + 2
@@ -274,6 +279,10 @@
 
         lax.fori_loop(1, parts, go, 0)
 
+    loads = [pltpu.make_async_copy(taps_far, taps_in, l_sem.at[0])]
+    loads += [pltpu.make_async_copy(one, two_, l_sem.at[1 + i]) for i, (one, two_) in enumerate(zip(far, near))]
+    for load in loads:
+        load.start()
     barrier = pltpu.get_barrier_semaphore()
 
     def greet(k, carry):
@@ -294,6 +303,8 @@
     edge_copy = remote(edge_send, edge, es_sem, er_sem, before)
     edge_copy.start()
 
+    for load in loads:
+        load.wait()
     band = lax.broadcasted_iota(jnp.int32, (held * count, LANES), 0) // count
     q = grid_q[...]
     slope = jnp.zeros((held * count, LANES), jnp.float32)
@@ -305,8 +316,30 @@
     scale = 1.0 / (count * LANES)
     phase_c = phase_c * scale
     phase_s = phase_s * scale
-    for source, high, low in ((a_in, a_h, a_l), (b_in, b_h, b_l)):
-        high[...], low[...] = split(source[...])
+    outer = turned.shape[0] // INNER
+    group = LANES // modes
+    both = 2 * modes
+    lane_group = lax.broadcasted_iota(jnp.int32, (outer, LANES), 1) // modes
+    for tile in range(both // group):
+        turned[...] = jnp.transpose(taps_in[tile * LANES : (tile + 1) * LANES, :])
+        for h in range(INNER // group):
+            lines = [turned[pl.ds(h * group + jj, outer, stride=INNER), :] for jj in range(group)]
+            for o in range(group):
+                value = None
+                for jj in range(group):
+                    turn = (jj - o) % group * modes
+                    line = pltpu.roll(lines[jj], turn, 1) if turn else lines[jj]
+                    value = line if value is None else jnp.where(lane_group == jj, line, value)
+                at_row = h * both * outer + (tile * group + o) * outer
+                a_f[at_row : at_row + outer, :] = value
+    tile_count = INNER // group
+    lines = []
+    for b in range(outer):
+        strips = [a_f[pl.ds(h * both * outer + b, both, stride=outer), :] for h in range(tile_count)]
+        lines.append(jnp.concatenate(strips, axis=1))
+        place = slice(b * both, (b + 1) * both)
+        a_h[place, :], a_l[place, :] = split(lines[-1])
+    b_h[...], b_l[...] = split(jnp.transpose(jnp.concatenate(lines, axis=0)))
     tc, ts = tw_c[...], tw_s[...]
     half_rows = held * count
 
@@ -336,7 +369,6 @@
     w = (vr * cosine - vi * sine, vr * sine + vi * cosine)
     full = wide * LANES
     ext = (rows + 1) * LANES
-    outer = a_in.shape[0] // (2 * modes)
     span = outer * INNER
 
     for c in range(2):
@@ -364,32 +396,35 @@
         misfit_out[c] = own
         m.append((own, jnp.where(keep, y[:, length:] - edge[c * modes : (c + 1) * modes, :], 0.0)))
 
-    zero = jnp.zeros((modes, LANES), jnp.float32)
-    own = [jnp.concatenate([part[0], zero], axis=1) for part in m]
+    m = [jnp.concatenate(part, axis=1) for part in m]
     for b in range(outer):
         base = b * 2 * modes
-        first = split(pltpu.roll(own[0], INNER * b + 1, 1))
-        second = split(pltpu.roll(own[1], INNER * b + 1, 1))
+        first = split(pltpu.roll(m[0], INNER * b + 1, 1))
+        second = split(pltpu.roll(m[1], INNER * b + 1, 1))
         for ref, one, two_ in ((mc_h, first[0], second[0]), (mc_l, first[1], second[1])):
             ref[base : base + modes, :ext] = one
             ref[base : base + modes, ext:] = two_
             ref[base + modes : base + 2 * modes, :ext] = two_
             ref[base + modes : base + 2 * modes, ext:] = -one
-    taps_own[...] = dot3((mc_h[...], mc_l[...]), (x_h[...], x_l[...]), (((1,), (1,)), ((), ())))
+    for start in (0, length, ext, ext + length):
+        shift = lax.broadcasted_iota(jnp.int32, (INNER * modes, LANES), 0) // modes
+        sample = lax.broadcasted_iota(jnp.int32, (INNER * modes, LANES), 1) + shift + (start % ext - span)
+        inside = (sample >= 0) & (sample < length)
+        for ref in (x_h, x_l):
+            strip = ref[:, start : start + LANES].astype(jnp.float32)
+            ref[:, start : start + LANES] = jnp.where(inside, strip, 0.0).astype(jnp.bfloat16)
+    coeffs = dot3((mc_h[...], mc_l[...]), (x_h[...], x_l[...]), (((1,), (1,)), ((), ())))
+    for b in range(outer):
+        for h in range(tile_count):
+            a_f[pl.ds(h * both * outer + b, both, stride=outer), :] = coeffs[b * both : (b + 1) * both, h * LANES : (h + 1) * LANES]
+    for h in range(tile_count):
+        taps_own[:, h * LANES : (h + 1) * LANES] = a_f[h * both * outer : (h + 1) * both * outer, :]
     half_size = taps_own.shape[0] // 2
     piece = half_size // chips
     swap = remote(rows_of(taps_own, 1 - core, half_size), rs1, c_ssem.at[0], c_rsem.at[0], sibling)
     swap.start()
 
-    joined = [jnp.concatenate(part, axis=1) for part in m]
-    for c in range(2):
-        for j in range(INNER):
-            moved = joined[c] if j == INNER - 1 else pltpu.roll(joined[c], ext - (INNER - 1 - j), 1)
-            high, low = split(moved)
-            place = (slice(j * modes, (j + 1) * modes), slice(c * ext, (c + 1) * ext))
-            y_h[place] = high
-            y_l[place] = low
-    prod[...] = dot3((b_h[...], b_l[...]), (y_h[...], y_l[...]))
+    grad_w[...] = dot3((b_h[...], b_l[...]), (mc_h[...], mc_l[...]))
 
     swap.wait_recv()
     half[...] = taps_own[pl.ds(pl.multiple_of(core * half_size, 8), half_size), :] + rs1[...]
@@ -403,19 +438,13 @@
 
     gr = jnp.zeros((modes, length), jnp.float32)
     gi = jnp.zeros((modes, length), jnp.float32)
-    for b in range(outer):
-        base = b * 2 * modes
-        rr = prod[base : base + modes, :ext] + prod[base + modes : base + 2 * modes, ext:]
-        ri = prod[base : base + modes, ext:] - prod[base + modes : base + 2 * modes, :ext]
-        shift = span - INNER - INNER * b
-        if shift:
-            rr = pltpu.roll(rr, ext - shift, 1)
-            ri = pltpu.roll(ri, ext - shift, 1)
-        gr = gr + rr[:, :length]
-        gi = gi + ri[:, :length]
+    for j in range(INNER):
+        rows_j = slice(j * modes, (j + 1) * modes)
+        gr = gr + pltpu.roll(grad_w[rows_j, :ext], ext - (span - j), 1)[:, :length]
+        gi = gi + pltpu.roll(grad_w[rows_j, ext:], ext - (span - j), 1)[:, :length]
     here = slice(LANES, LANES + length)
     wr, wi, cosine, sine = w[0][:, here], w[1][:, here], cosine[:, here], sine[:, here]
-    pull = dot3(split(coupling_t[...]), split(gi * wr - gr * wi)) * 2.0
+    pull = dot3(split(jnp.transpose(coupling[...])), split(gi * wr - gr * wi)) * 2.0
     vr = gr * cosine + gi * sine + vr[:, here] * pull
     vi = gi * cosine - gr * sine + vi[:, here] * pull
     for c, value in ((0, vr), (1, vi)):
@@ -437,11 +466,20 @@
     total = rs2[:piece, :]
     for k in range(1, chips):
         total = total + rs2[k * piece : (k + 1) * piece, :]
-    mine_sum[...] = total * (1.0 / math.sqrt(count * LANES))
+    total = total * (1.0 / math.sqrt(count * LANES))
+    for h in range(INNER // group):
+        for jj in range(group):
+            value = None
+            for o in range(group):
+                turn = (o - jj) % group * modes
+                line = total[o * outer : (o + 1) * outer, h * LANES : (h + 1) * LANES]
+                line = pltpu.roll(line, turn, 1) if turn else line
+                value = line if value is None else jnp.where(lane_group == o, line, value)
+            mine_sum[pl.ds(h * group + jj, outer, stride=INNER), :] = value
     base = 1 + chips
 
     def slot(c_, k_):
-        return rows_of(gathered, c_ * chips + k_, piece)
+        return rows_of(gathered, c_ * chips + k_, span)
 
     def spread(k, carry):
         other = lax.rem(chip + k, chips)
@@ -451,7 +489,7 @@
     lax.fori_loop(1, chips, spread, 0)
     base2 = base + chips
     remote(mine_sum, slot(core, chip), c_ssem.at[base2 + chip], c_rsem.at[base2 + chip], sibling).start()
-    gathered[pl.ds(pl.multiple_of((core * chips + chip) * piece, 8), piece), :] = mine_sum[...]
+    gathered[pl.ds(pl.multiple_of((core * chips + chip) * span, 8), span), :] = mine_sum[...]
 
     arrive(3, send4, recv4, block)
     for c in range(2):
@@ -471,7 +509,8 @@
         return carry
 
     lax.fori_loop(0, chips, collect, 0)
-    tap_out[...] = gathered[...]
+    for k in range(parts):
+        tap_out[k * LANES : (k + 1) * LANES, :] = jnp.transpose(gathered[k * span : (k + 1) * span, :])
 
     edge_copy.wait_send()
     swap.wait_send()
@@ -508,9 +547,6 @@
     plain = rows * parts * held * 2
     ext = (rows + 1) * LANES
     chips = parts // 2
-    pieces = taps.reshape(2, modes, modes, outer, INNER)
-    forward = pieces.transpose(3, 0, 1, 4, 2).reshape(outer * 2 * modes, INNER * modes)
-    backward = pieces.transpose(3, 0, 2, 4, 1).reshape(outer * 2 * modes, INNER * modes)
     size = outer * 2 * modes
     cols = INNER * modes
     tables_ = [jnp.asarray(table) for table in dft_tables(parts, rows, held)]
@@ -523,29 +559,32 @@
         out_shape=(
             jax.ShapeDtypeStruct((2, modes, length), f32),
             jax.ShapeDtypeStruct((2, modes, length), f32),
-            jax.ShapeDtypeStruct((size, cols), f32),
+            jax.ShapeDtypeStruct((2 * modes * modes, span), f32),
         ),
-        in_specs=[vmem] * 6 + [smem] * 2 + [vmem] * len(tables_),
+        in_specs=[vmem] * 3 + [smem] * 2 + [pl.BlockSpec(memory_space=pltpu.HBM)] * (1 + len(tables_)),
         out_specs=(vmem, vmem, vmem),
         scratch_shapes=[
+            pltpu.VMEM((2 * modes * modes, span), f32),
+            *[pltpu.VMEM(table.shape, table.dtype) for table in tables_],
             field(plain), field(plain), field(wide), field(wide), field(plain), field(plain), field(plain), field(plain),
             field(2 * modes), field(2 * modes),
             pltpu.VMEM((size, cols), f32), pltpu.VMEM((size // 2, cols), f32), pltpu.VMEM((size // 2, cols), f32),
-            pltpu.VMEM((size // 2, cols), f32), pltpu.VMEM((size // parts, cols), f32), pltpu.VMEM((size, cols), f32),
+            pltpu.VMEM((size // 2, cols), f32), pltpu.VMEM((span, LANES), f32), pltpu.VMEM((parts * span, LANES), f32),
+            pltpu.VMEM((span, LANES), f32), pltpu.VMEM((cols // LANES * size, LANES), f32),
             pltpu.VMEM((size, cols), bf16), pltpu.VMEM((size, cols), bf16),
-            pltpu.VMEM((size, cols), bf16), pltpu.VMEM((size, cols), bf16),
+            pltpu.VMEM((cols, size), bf16), pltpu.VMEM((cols, size), bf16),
             pltpu.VMEM((cols, 2 * ext), bf16), pltpu.VMEM((cols, 2 * ext), bf16),
             pltpu.VMEM((size, 2 * ext), f32),
             pltpu.VMEM((size, 2 * ext), bf16), pltpu.VMEM((size, 2 * ext), bf16),
-            pltpu.VMEM((cols, 2 * ext), bf16), pltpu.VMEM((cols, 2 * ext), bf16),
+            pltpu.VMEM((cols, 2 * ext), f32),
             pltpu.SemaphoreType.DMA((4, parts)), pltpu.SemaphoreType.DMA((4, parts)),
             pltpu.SemaphoreType.DMA, pltpu.SemaphoreType.DMA,
             pltpu.SemaphoreType.DMA((1 + 3 * chips,)), pltpu.SemaphoreType.DMA((1 + 3 * chips,)),
+            pltpu.SemaphoreType.DMA((1 + len(tables_),)),
         ],
         compiler_params=pltpu.CompilerParams(collective_id=0, has_side_effects=True, vmem_limit_bytes=48 * 1024 * 1024),
-    )(launch, target, forward, backward, coupling, coupling.T, delay, curv, *tables_)
-    tap = tap.reshape(outer, 2, modes, INNER, modes).transpose(1, 2, 4, 0, 3).reshape(taps.shape)
-    return misfit, launch_grad, tap
+    )(launch, target, coupling, delay, curv, taps.reshape(2 * modes * modes, span), *tables_)
+    return misfit, launch_grad, tap.reshape(taps.shape)
 
 
 def fits(launch, taps, parts):
@@ -557,8 +596,10 @@
         and modes % 16 == 0
         and length % LANES == 0
         and length * parts == WIN
-        and taps.shape[-1] % INNER == 0
-        and taps.shape[-1] < LANES
+        and LANES % modes == 0
+        and INNER % (LANES // modes) == 0
+        and taps.shape[-1] == INNER * 8
+        and 2 * modes == parts * (LANES // modes)
         and (2 * (modes // parts) * (length // LANES)) % 8 == 0
         and (2 * (modes // parts) * (length // LANES + 2)) % 8 == 0
     )

time: 72.9 us -> 71.9 us (0.986)
  local copies, waits for them, and re-layouts: 22.1 us -> 18.3 us
  Pallas kernels: 49.6 us -> 52.3 us
    unnamed x43 -> x41, local copies, waits for them, and re-layouts: 11.6 us -> 18.3 us
    reshape x4 -> x0, local copies, waits for them, and re-layouts: 6.54 us -> none  [the longest x1 2.31 us: fused(): pieces.transpose(3, 0, 2, 4, 1).reshape(outer * 2 * modes, INNER * modes)]
    transpose x2 -> x0, local copies, waits for them, and re-layouts: 3.93 us -> none  [the longest x1 2.38 us: fused(): pieces.transpose(3, 0, 2, 4, 1).reshape(outer * 2 * modes, INNER * modes)]
    pallas_call x1, Pallas kernels: 49.6 us -> 52.3 us  [fused(): pl.pallas_call(functools.partial(kernel, parts), out_shape=(jax.ShapeDtyp...]
where the time goes in v1:
time: 71.9 us; the launch traced here: 71.3 us
  Pallas kernels  52.3 us (73%)
  local copies, waits for them, and re-layouts  18.3 us (25%)
    pallas_call x1, Pallas kernels, fused(): pl.pallas_call(functools.partial(kernel, parts), out_shape=(jax.ShapeDtyp...  52.3 us
    unnamed x41, local copies, waits for them, and re-layouts  18.3 us

profile of v1, /device:TPU:1, one launch (start us, length us, event | category | flops | bytes accessed | tf_op | source)
XLA Modules:
  0.0 71.3 jit_solution(14509989083775542171)
XLA Ops:
  0.6 0.0 copy-start.18
  0.7 0.6 copy-done.18
  1.3 0.0 copy-done.17
  1.3 1.2 %copy-done = f32[2,32,32,64]{3,2,1,0:T(8,128)S(1)} copy-done((f32[2,32,32,64]{3,2,1,0:T(8,128)S(1)}, f32[2,32,32,64]{3,2,1,0:T(8,128)}, u32[]{:S(2)}) %copy-start) | copy-done | bytes 524312
  2.5 0.9 %copy-done.1 = bf16[384,256]{1,0:T(8,128)(2,1)S(1)} copy-done((bf16[384,256]{1,0:T(8,128)(2,1)S(1)}, bf16[384,256]{1,0:T(8,128)(2,1)}, u32[]{:S(2)}) %copy-start.1) | copy-done | bytes 196632
  3.5 0.9 %copy-done.2 = bf16[384,256]{1,0:T(8,128)(2,1)S(1)} copy-done((bf16[384,256]{1,0:T(8,128)(2,1)S(1)}, bf16[384,256]{1,0:T(8,128)(2,1)}, u32[]{:S(2)}) %copy-start.2) | copy-done | bytes 196632
  4.4 0.9 %copy-done.3 = f32[2,32,512]{2,1,0:T(8,128)S(1)} copy-done((f32[2,32,512]{2,1,0:T(8,128)S(1)}, f32[2,32,512]{2,1,0:T(8,128)}, u32[]{:S(2)}) %copy-start.3) | copy-done | bytes 131096
  5.3 0.9 %copy-done.4 = f32[2,32,512]{2,1,0:T(8,128)S(1)} copy-done((f32[2,32,512]{2,1,0:T(8,128)S(1)}, f32[2,32,512]{2,1,0:T(8,128)}, u32[]{:S(2)}) %copy-start.4) | copy-done | bytes 131096
  6.2 0.9 %copy-done.5 = bf16[256,256]{1,0:T(8,128)(2,1)S(1)} copy-done((bf16[256,256]{1,0:T(8,128)(2,1)S(1)}, bf16[256,256]{1,0:T(8,128)(2,1)}, u32[]{:S(2)}) %copy-start.5) | copy-done | bytes 131096
  7.1 0.9 %copy-done.6 = bf16[256,256]{1,0:T(8,128)(2,1)S(1)} copy-done((bf16[256,256]{1,0:T(8,128)(2,1)S(1)}, bf16[256,256]{1,0:T(8,128)(2,1)}, u32[]{:S(2)}) %copy-start.6) | copy-done | bytes 131096
  8.0 0.9 %copy-done.7 = bf16[256,256]{1,0:T(8,128)(2,1)S(1)} copy-done((bf16[256,256]{1,0:T(8,128)(2,1)S(1)}, bf16[256,256]{1,0:T(8,128)(2,1)}, u32[]{:S(2)}) %copy-start.7) | copy-done | bytes 131096
  8.9 0.9 %copy-done.8 = bf16[256,256]{1,0:T(8,128)(2,1)S(1)} copy-done((bf16[256,256]{1,0:T(8,128)(2,1)S(1)}, bf16[256,256]{1,0:T(8,128)(2,1)}, u32[]{:S(2)}) %copy-start.8) | copy-done | bytes 131096
  9.8 0.9 %copy-done.9 = bf16[256,256]{1,0:T(8,128)(2,1)S(1)} copy-done((bf16[256,256]{1,0:T(8,128)(2,1)S(1)}, bf16[256,256]{1,0:T(8,128)(2,1)}, u32[]{:S(2)}) %copy-start.9) | copy-done | bytes 131096
  10.7 0.9 %copy-done.10 = bf16[256,256]{1,0:T(8,128)(2,1)S(1)} copy-done((bf16[256,256]{1,0:T(8,128)(2,1)S(1)}, bf16[256,256]{1,0:T(8,128)(2,1)}, u32[]{:S(2)}) %copy-start.10) | copy-done | bytes 131096
  11.6 0.9 %copy-done.11 = bf16[256,256]{1,0:T(8,128)(2,1)S(1)} copy-done((bf16[256,256]{1,0:T(8,128)(2,1)S(1)}, bf16[256,256]{1,0:T(8,128)(2,1)}, u32[]{:S(2)}) %copy-start.11) | copy-done | bytes 131096
  12.5 0.9 %copy-done.12 = bf16[256,256]{1,0:T(8,128)(2,1)S(1)} copy-done((bf16[256,256]{1,0:T(8,128)(2,1)S(1)}, bf16[256,256]{1,0:T(8,128)(2,1)}, u32[]{:S(2)}) %copy-start.12) | copy-done | bytes 131096
  13.4 0.8 %copy-done.13 = f32[128,128]{1,0:T(8,128)S(1)} copy-done((f32[128,128]{1,0:T(8,128)S(1)}, f32[128,128]{1,0:T(8,128)}, u32[]{:S(2)}) %copy-start.13) | copy-done | bytes 65560
  14.3 0.8 %copy-done.14 = f32[128,128]{1,0:T(8,128)S(1)} copy-done((f32[128,128]{1,0:T(8,128)S(1)}, f32[128,128]{1,0:T(8,128)}, u32[]{:S(2)}) %copy-start.14) | copy-done | bytes 65560
  15.1 0.8 %copy-done.15 = f32[128,128]{1,0:T(8,128)S(1)} copy-done((f32[128,128]{1,0:T(8,128)S(1)}, f32[128,128]{1,0:T(8,128)}, u32[]{:S(2)}) %copy-start.15) | copy-done | bytes 65560
  16.0 0.7 %copy-done.16 = f32[32,32]{1,0:T(8,128)S(1)} copy-done((f32[32,32]{1,0:T(8,128)S(1)}, f32[32,32]{1,0:T(8,128)}, u32[]{:S(2)}) %copy-start.16) | copy-done | bytes 4120
  16.7 52.3 %shard_map.202 = (f32[2,32,512]{2,1,0:T(8,128)S(1)}, f32[2,32,512]{2,1,0:T(8,128)S(1)}, f32[2048,64]{1,0:T(8,128)S(1)}) custom-call(f32[2,32,512]{2,1,0:T(8,128)S(1)} %copy-done.3, f32[2,32,512]{2,1,0:T(8,128)S(1)} %copy-done.4, f32[32,32]{1,0:T(8,128)S(1)} %copy-done.16, f32[32]{0:T(128)S(1)} %copy-done.17, f32[32]{0:T(128)S(1)} %copy-done.18, ...), custom_call_target="tpu_custom_call" | custom-call | tf_op jit(solution)/shard_map/pallas_call | solution.py:557
  69.0 0.7 copy.25
  69.7 0.7 copy.26
  70.3 1.0 %copy.27 = f32[2,32,32,64]{3,2,1,0:T(8,128)} copy(f32[2,32,32,64]{3,2,1,0:T(8,128)S(1)} %bitcast.3) | data formatting | bytes 1048576
  (18 shorter events, 0.0 us)
Async XLA Ops:
  0.6 0.7 copy-start.18
  0.6 0.7 copy-start.17
  1.3 1.2 %copy-start = (f32[2,32,32,64]{3,2,1,0:T(8,128)S(1)}, f32[2,32,32,64]{3,2,1,0:T(8,128)}, u32[]{:S(2)}) copy-start(f32[2,32,32,64]{3,2,1,0:T(8,128)} %param.21) | copy-start | bytes 1572868
  2.5 0.9 %copy-start.1 = (bf16[384,256]{1,0:T(8,128)(2,1)S(1)}, bf16[384,256]{1,0:T(8,128)(2,1)}, u32[]{:S(2)}) copy-start(bf16[384,256]{1,0:T(8,128)(2,1)} %constant.31.clone.rest_5_) | copy-start | bytes 589828
  3.5 0.9 %copy-start.2 = (bf16[384,256]{1,0:T(8,128)(2,1)S(1)}, bf16[384,256]{1,0:T(8,128)(2,1)}, u32[]{:S(2)}) copy-start(bf16[384,256]{1,0:T(8,128)(2,1)} %constant.30.clone.rest_4_) | copy-start | bytes 589828
  4.4 0.9 %copy-start.3 = (f32[2,32,512]{2,1,0:T(8,128)S(1)}, f32[2,32,512]{2,1,0:T(8,128)}, u32[]{:S(2)}) copy-start(f32[2,32,512]{2,1,0:T(8,128)} %launch.1) | copy-start | bytes 393220
  5.3 0.9 %copy-start.4 = (f32[2,32,512]{2,1,0:T(8,128)S(1)}, f32[2,32,512]{2,1,0:T(8,128)}, u32[]{:S(2)}) copy-start(f32[2,32,512]{2,1,0:T(8,128)} %target.1) | copy-start | bytes 393220
  6.2 0.9 %copy-start.5 = (bf16[256,256]{1,0:T(8,128)(2,1)S(1)}, bf16[256,256]{1,0:T(8,128)(2,1)}, u32[]{:S(2)}) copy-start(bf16[256,256]{1,0:T(8,128)(2,1)} %constant.35.clone.rest_9_) | copy-start | bytes 393220
  7.1 0.9 %copy-start.6 = (bf16[256,256]{1,0:T(8,128)(2,1)S(1)}, bf16[256,256]{1,0:T(8,128)(2,1)}, u32[]{:S(2)}) copy-start(bf16[256,256]{1,0:T(8,128)(2,1)} %constant.34.clone.rest_8_) | copy-start | bytes 393220
  8.0 0.9 %copy-start.7 = (bf16[256,256]{1,0:T(8,128)(2,1)S(1)}, bf16[256,256]{1,0:T(8,128)(2,1)}, u32[]{:S(2)}) copy-start(bf16[256,256]{1,0:T(8,128)(2,1)} %constant.33.clone.rest_7_) | copy-start | bytes 393220
  8.9 0.9 %copy-start.8 = (bf16[256,256]{1,0:T(8,128)(2,1)S(1)}, bf16[256,256]{1,0:T(8,128)(2,1)}, u32[]{:S(2)}) copy-start(bf16[256,256]{1,0:T(8,128)(2,1)} %constant.32.clone.rest_6_) | copy-start | bytes 393220
  9.8 0.9 %copy-start.9 = (bf16[256,256]{1,0:T(8,128)(2,1)S(1)}, bf16[256,256]{1,0:T(8,128)(2,1)}, u32[]{:S(2)}) copy-start(bf16[256,256]{1,0:T(8,128)(2,1)} %constant.29.clone.rest_3_) | copy-start | bytes 393220
  10.7 0.9 %copy-start.10 = (bf16[256,256]{1,0:T(8,128)(2,1)S(1)}, bf16[256,256]{1,0:T(8,128)(2,1)}, u32[]{:S(2)}) copy-start(bf16[256,256]{1,0:T(8,128)(2,1)} %constant.28.clone.rest_2_) | copy-start | bytes 393220
  11.6 0.9 %copy-start.11 = (bf16[256,256]{1,0:T(8,128)(2,1)S(1)}, bf16[256,256]{1,0:T(8,128)(2,1)}, u32[]{:S(2)}) copy-start(bf16[256,256]{1,0:T(8,128)(2,1)} %constant.27.clone.rest_1_) | copy-start | bytes 393220
  12.5 0.9 %copy-start.12 = (bf16[256,256]{1,0:T(8,128)(2,1)S(1)}, bf16[256,256]{1,0:T(8,128)(2,1)}, u32[]{:S(2)}) copy-start(bf16[256,256]{1,0:T(8,128)(2,1)} %constant.26.clone.rest_0_) | copy-start | bytes 393220
  13.4 0.8 %copy-start.13 = (f32[128,128]{1,0:T(8,128)S(1)}, f32[128,128]{1,0:T(8,128)}, u32[]{:S(2)}) copy-start(f32[128,128]{1,0:T(8,128)} %constant.38.clone.rest_12_) | copy-start | bytes 196612
  14.3 0.8 %copy-start.14 = (f32[128,128]{1,0:T(8,128)S(1)}, f32[128,128]{1,0:T(8,128)}, u32[]{:S(2)}) copy-start(f32[128,128]{1,0:T(8,128)} %constant.37.clone.rest_11_) | copy-start | bytes 196612
  15.1 0.8 %copy-start.15 = (f32[128,128]{1,0:T(8,128)S(1)}, f32[128,128]{1,0:T(8,128)}, u32[]{:S(2)}) copy-start(f32[128,128]{1,0:T(8,128)} %constant.36.clone.rest_10_) | copy-start | bytes 196612
  16.0 0.7 %copy-start.16 = (f32[32,32]{1,0:T(8,128)S(1)}, f32[32,32]{1,0:T(8,128)}, u32[]{:S(2)}) copy-start(f32[32,32]{1,0:T(8,128)} %coupling.1) | copy-start | bytes 12292
